TPU v7x, 1024 devices: a whole 4x4x32 slice. The times are simulated.
1024 devices in a mesh: gx: 32 (over z), gy: 4 (over x), gz: 8 (over y, core).
Axes of the slice: x: 4, y: 4, z: 32, core: 2. Of those that a mesh axis runs over, the one named last changes fastest.
Arguments:
- right_side: float32 [64, 32, 1024], P('gx', 'gy', 'gz'), may hold values from -8 to 8
- stencil: float32 [27, 64, 32, 1024], P(None, 'gx', 'gy', 'gz'), may hold values from -2 to 64, as said below
- cool_table: float32 [256], replicated, may hold values from 0.25 to 4
- cool_bin: int32 [64, 32, 1024], P('gx', 'gy', 'gz'), may hold values from 0 to 254
- cool_frac: float32 [64, 32, 1024], P('gx', 'gy', 'gz'), may hold values from 0 to 1
Outputs:
- solution_field: float32 [64, 32, 1024], P('gx', 'gy', 'gz')
- residual: float32 [64, 32, 1024], P('gx', 'gy', 'gz')
Inputs may be any that keep to these rules, and one draw needn't show every extreme that they name: stencil is symmetric: stencil[26 - index] at a cell equals stencil[index] at the cell's neighbour at that index's offset; off-centre entries are not positive and stencil[13] is about 1 plus the sum of their magnitudes.
All inputs are finite; a program needn't handle non-finite values.
Results may differ from a plain program's by a relative error of at most 0.0003.
Values sent between devices are 32-bit elements; how exact they have to be, the bound alone decides.
A program may use at most 32 MiB of HBM per device.

v0:
```python
import jax
import jax.numpy as jnp
from jax import lax
from jax.sharding import PartitionSpec as P

ITERS = 3


def padded_2(block, sides, width):
    for axis, dim in sides:
        count = lax.axis_size(axis)
        forward = [(i, i + 1) for i in range(count - 1)]
        forward.append((count - 1, 0))
        backward = [(target, source) for source, target in forward]
        low = lax.ppermute(
            lax.slice_in_dim(block, block.shape[dim] - width, None, axis=dim), axis, forward
        )
        high = lax.ppermute(lax.slice_in_dim(block, 0, width, axis=dim), axis, backward)
        block = jnp.concatenate([low, block, high], axis=dim)
    return block


def cooling_slope(cool_table, cool_bin, cool_frac):
    nbins = cool_table.shape[0]
    table_next = jnp.concatenate([cool_table[1:], cool_table[-1:]])
    levels = lax.broadcasted_iota(jnp.int32, (1, nbins), 1)
    bin_rows = cool_bin.reshape(-1, cool_bin.shape[-1])
    frac_rows = cool_frac.reshape(-1, cool_frac.shape[-1])

    def one_row(pair):
        row_bins, row_frac = pair
        hit = row_bins[:, None] == levels
        lower = jnp.sum(jnp.where(hit, cool_table[None, :], 0.0), axis=1)
        upper = jnp.sum(jnp.where(hit, table_next[None, :], 0.0), axis=1)
        return lower * (1.0 - row_frac) + upper * row_frac

    slope = lax.map(one_row, (bin_rows, frac_rows), batch_size=16)
    return slope.reshape(cool_bin.shape)


def neighbours(field):
    return padded_2(field, (("gx", 0), ("gy", 1), ("gz", 2)), 1)


def operate(field, stencil, slope):
    padded = neighbours(field)
    size_x, size_y, size_z = field.shape
    total = slope * field
    for index in range(27):
        start_x = index // 9
        start_y = index // 3 % 3
        start_z = index % 3
        moved = padded[
            start_x : start_x + size_x, start_y : start_y + size_y, start_z : start_z + size_z
        ]
        total = total + stencil[index] * moved
    return total


def squares(residual):
    return lax.psum(jnp.sum(residual * residual), ("gx", "gy", "gz"))


def local(right_side, stencil, cool_table, cool_bin, cool_frac):
    slope = cooling_slope(cool_table, cool_bin, cool_frac)
    solution_field = jnp.zeros_like(right_side)
    residual = right_side
    direction = right_side
    norm_now = squares(residual)
    for step in range(ITERS):
        image = operate(direction, stencil, slope)
        alpha = norm_now / lax.psum(jnp.sum(direction * image), ("gx", "gy", "gz"))
        solution_field = solution_field + alpha * direction
        residual = residual - alpha * image
        if step + 1 < ITERS:
            norm_next = squares(residual)
            direction = residual + norm_next / norm_now * direction
            norm_now = norm_next
    return (solution_field, residual)


def solution(mesh):
    in_specs = (
        P("gx", "gy", "gz"),
        P(None, "gx", "gy", "gz"),
        P(),
        P("gx", "gy", "gz"),
        P("gx", "gy", "gz"),
    )
    out_specs = (P("gx", "gy", "gz"), P("gx", "gy", "gz"))
    return jax.shard_map(local, mesh=mesh, in_specs=in_specs, out_specs=out_specs, check_vma=False)
```

profile of v0, /device:TPU:1, one launch (start us, length us, event | category | flops | bytes accessed | tf_op | source)
XLA Modules:
  0.0 865.5 jit_solution(7834813332768454845)
XLA Ops:
  1.4 4.4 collective-permute-start
  5.7 16.8 %collective-permute-start.1 = (f32[1,8,128]{2,1,0:T(8,128)S(1)}, f32[1,8,128]{2,1,0:T(8,128)S(1)}, u32[]{:S(2)}, u32[]{:S(2)}) collective-permute-start(f32[1,8,128]{2,1,0:T(8,128)S(1)} %get-tuple-element.59), channel_id=1, source_target_pairs={{32,0},{64,32},{96,64},{128,96},{160,128},{192,160},{224,192},{256... | collective-permute-start | bytes 12296 | tf_op jit(solution)/shard_map/ppermute | solution.py:18
  25.2 3.1 collective-permute-start.2
  28.4 3.4 collective-permute-start.3
  32.8 3.6 collective-permute-start.4
  37.6 2.1 collective-permute-done.5
  40.6 156.1 %all-reduce = (f32[]{:T(128)}, f32[]{:T(128)}) all-reduce(f32[]{:T(128)} %get-tuple-element.17, f32[]{:T(128)} %get-tuple-element.16), channel_id=1, replica_groups=mesh['gx'=32,'gy'=4,'gz'=8] {'gx','gy','gz'}, use_global_device_ids=true, to_apply=%region_1.2 | all-reduce | flops 2 | bytes 16 | tf_op jit(solution)/shard_map/psum | solution.py:61
  198.6 150.5 %psum.44 = f32[]{:T(128)} all-reduce(f32[]{:T(128)} %multiply_reduce_fusion.3), channel_id=1, replica_groups=mesh['gx'=32,'gy'=4,'gz'=8] {'gx','gy','gz'}, use_global_device_ids=true, to_apply=%region_7.8 | all-reduce | flops 1 | bytes 8 | tf_op jit(solution)/shard_map/psum | solution.py:61
  350.4 3.7 collective-permute-start.6
  354.1 2.8 collective-permute-start.7
  358.4 2.4 collective-permute-start.8
  360.8 4.1 collective-permute-start.9
  365.7 3.6 collective-permute-start.10
  370.3 2.6 collective-permute-done.11
  373.7 156.3 %psum.45 = f32[]{:T(128)} all-reduce(f32[]{:T(128)} %get-tuple-element.33), channel_id=1, replica_groups=mesh['gx'=32,'gy'=4,'gz'=8] {'gx','gy','gz'}, use_global_device_ids=true, to_apply=%region_9.10 | all-reduce | flops 1 | bytes 8 | tf_op jit(solution)/shard_map/psum | solution.py:72
  532.0 150.5 %psum.46 = f32[]{:T(128)} all-reduce(f32[]{:T(128)} %get-tuple-element.31), channel_id=1, replica_groups=mesh['gx'=32,'gy'=4,'gz'=8] {'gx','gy','gz'}, use_global_device_ids=true, to_apply=%region_11.12 | all-reduce | flops 1 | bytes 8 | tf_op jit(solution)/shard_map/psum | solution.py:61
  683.9 3.7 collective-permute-start.12
  687.6 2.8 collective-permute-start.13
  690.4 1.5 collective-permute-done.13
  692.0 2.3 collective-permute-start.14
  694.2 4.2 collective-permute-start.15
  699.3 3.4 collective-permute-start.16
  703.7 2.6 collective-permute-done.17
  707.2 156.4 %psum.47 = f32[]{:T(128)} all-reduce(f32[]{:T(128)} %get-tuple-element.29), channel_id=1, replica_groups=mesh['gx'=32,'gy'=4,'gz'=8] {'gx','gy','gz'}, use_global_device_ids=true, to_apply=%region_13.14 | all-reduce | flops 1 | bytes 8 | tf_op jit(solution)/shard_map/psum | solution.py:72
  (57 shorter events, 15.1 us)
Async XLA Ops:
  0.6 35.7 %copy-start.4 = (f32[256]{0:T(256)S(1)}, f32[256]{0:T(256)}, u32[]{:S(2)}) copy-start(f32[256]{0:T(256)} %param.7) | copy-start | bytes 3076
  0.6 35.7 %copy-start.3 = (s32[2,8,128]{2,1,0:T(8,128)S(1)}, s32[2,8,128]{2,1,0:T(8,128)}, u32[]{:S(2)}) copy-start(s32[2,8,128]{2,1,0:T(8,128)} %param.8) | copy-start | bytes 24580
  1.4 23.2 %collective-permute-start = (f32[1,8,128]{2,1,0:T(8,128)S(1)}, f32[1,8,128]{2,1,0:T(8,128)S(1)}, u32[]{:S(2)}, u32[]{:S(2)}) collective-permute-start(f32[1,8,128]{2,1,0:T(8,128)S(1)} %get-tuple-element.60), channel_id=1, source_target_pairs={{0,32},{32,64},{64,96},{96,128},{128,160},{160,192},{192,224},{224... | collective-permute-start | bytes 12296 | tf_op jit(solution)/shard_map/ppermute | solution.py:15
  5.7 19.5 %collective-permute-start.1 = (f32[1,8,128]{2,1,0:T(8,128)S(1)}, f32[1,8,128]{2,1,0:T(8,128)S(1)}, u32[]{:S(2)}, u32[]{:S(2)}) collective-permute-start(f32[1,8,128]{2,1,0:T(8,128)S(1)} %get-tuple-element.59), channel_id=1, source_target_pairs={{32,0},{64,32},{96,64},{128,96},{160,128},{192,160},{224,192},{256... | collective-permute-start | bytes 12296 | tf_op jit(solution)/shard_map/ppermute | solution.py:18
  25.2 7.2 collective-permute-start.2
  28.4 4.3 collective-permute-start.3
  32.5 7.3 copy-start
  32.5 7.3 copy-start.1
  32.5 7.4 copy-start.2
  32.8 4.8 collective-permute-start.4
  36.4 3.3 collective-permute-start.5
  350.4 6.5 collective-permute-start.6
  354.1 4.4 collective-permute-start.7
  358.4 6.5 collective-permute-start.8
  360.8 4.8 collective-permute-start.9
  365.7 4.6 collective-permute-start.10
  369.3 3.6 collective-permute-start.11
  683.9 6.5 collective-permute-start.12
  687.6 4.4 collective-permute-start.13
  692.0 6.5 collective-permute-start.14
  694.2 5.0 collective-permute-start.15
  699.3 4.5 collective-permute-start.16
  702.7 3.6 collective-permute-start.17
where the time goes:
time: 867 us; the launch traced here: 865 us
  blocking collectives  770 us (89%)
  starting transfers between devices  64.2 us (7%)
  waiting for transfers between devices  14 us (2%)
    psum x3, blocking collectives, squares(): return lax.psum(jnp.sum(residual * residual), ('gx', 'gy', 'gz'))  457 us
    psum x2, blocking collectives, local(): alpha = norm_now / lax.psum(jnp.sum(direction * image), ('gx', 'gy', 'gz'))  313 us
    ppermute x9, starting transfers between devices, padded_2(): lax.ppermute(lax.slice_in_dim(block, 0, width, axis=dim), axis, backward)  34.2 us
    ppermute x9, starting transfers between devices, padded_2(): lax.ppermute(lax.slice_in_dim(block, block.shape[dim] - width, None, axis...  30 us
  transfers between devices with their start and end apart: 18, of which 10 were waited for; matrix products, arithmetic and copies ran while one was open for 1% of the time, Pallas kernels for 0%

commit v1 on v0

v1 whole, which is shorter than its diff:
```python
import functools
import jax
import jax.numpy as jnp
from jax import lax
from jax.experimental import pallas as pl
from jax.experimental.pallas import tpu as pltpu
from jax.sharding import PartitionSpec as P

MESH = pl.DeviceIdType.MESH
GX, GY, GZ = 32, 4, 8
PLANE = GY * GZ
SHIFT = 4.5
OFFSETS = [
    (a, b, c)
    for a in (-1, 0, 1)
    for b in (-1, 0, 1)
    for c in (-1, 0, 1)
    if (a, b, c) != (0, 0, 0)
]


def two_sum(a, b):
    total = a + b
    part = total - a
    return total, (a - (total - part)) + (b - part)


def pair_add(x, y):
    total, error = two_sum(x[0], y[0])
    error = error + (x[1] + y[1])
    high = total + error
    return high, error - (high - total)


def halves(a):
    big = a * 4097.0
    high = big - (big - a)
    return high, a - high


def pair_minus_scaled(x, y, scale, scale_halves):
    product = y[0] * scale
    high, low = halves(y[0])
    scale_high, scale_low = scale_halves
    error = high * scale_high - product
    error = error + high * scale_low
    error = error + low * scale_high
    error = error + low * scale_low
    error = error + y[1] * scale
    return pair_add(x, (-product, -error))


def conjugate(moments):
    tau = moments[1][0] / moments[0][0]
    tau_halves = halves(tau)
    level = list(moments)
    shifted = [level[0][0]]
    while len(level) > 1:
        level = [
            pair_minus_scaled(level[k + 1], level[k], tau, tau_halves)
            for k in range(len(level) - 1)
        ]
        shifted.append(level[0][0])
    m = shifted
    s = tau + SHIFT

    def form(p, q):
        total = None
        for i, u in enumerate(p):
            inner = None
            for j, w in enumerate(q):
                term = w * m[i + j]
                inner = term if inner is None else inner + term
            total = u * inner if total is None else total + u * inner
        return total

    def image_of(p):
        out = [s * p[0]]
        for i in range(1, len(p)):
            out.append(p[i - 1] + s * p[i])
        out.append(p[-1])
        return out

    bottom = s * m[0] + m[1]
    alpha = m[0] / bottom
    x = [alpha]
    r = [m[1] / bottom, -alpha]
    norm = form(r, r)
    beta = norm / m[0]
    d = [r[0] + beta, r[1]]
    for step in (1, 2):
        image = image_of(d)
        alpha = norm / form(d, image)
        x = [x[i] + alpha * d[i] if i < len(x) else alpha * d[i] for i in range(len(d))]
        r = [r[i] - alpha * image[i] if i < len(r) else -alpha * image[i] for i in range(len(image))]
        if step == 1:
            new = form(r, r)
            beta = new / norm
            d = [r[i] + beta * d[i] if i < len(d) else r[i] for i in range(len(r))]
            norm = new
    return tau, x, r


def kernel(
    rhs_hbm, stencil_hbm, table_hbm, bin_hbm, frac_hbm, x_out, r_out,
    st, halo, table, bins, frac, plane_rows, line_rows,
    in_sem, send_sem, halo_sem, plane_sem, line_sem, halo_bytes,
):
    gx, gy, gz = lax.axis_index("gx"), lax.axis_index("gy"), lax.axis_index("gz")

    def at(dx, dy, dz):
        return (
            lax.rem(gx + (dx + GX), GX),
            lax.rem(gy + (dy + GY), GY),
            lax.rem(gz + (dz + GZ), GZ),
        )

    loads = [
        pltpu.make_async_copy(rhs_hbm, halo.at[0, 0:2, 0, 0:8, :], in_sem.at[0]),
        pltpu.make_async_copy(stencil_hbm, st, in_sem.at[1]),
        pltpu.make_async_copy(table_hbm, table, in_sem.at[2]),
        pltpu.make_async_copy(bin_hbm, bins, in_sem.at[3]),
        pltpu.make_async_copy(frac_hbm, frac, in_sem.at[4]),
    ]
    for load in loads:
        load.start()

    plane_offsets = [(0, b, c) for b in range(GY) for c in range(GZ) if (b, c) != (0, 0)]
    line_offsets = [(a, 0, 0) for a in [16] + [k * e for k in range(15, 0, -1) for e in (1, -1)]]
    partners = line_offsets + [o for o in OFFSETS if o[0] != 0 and (o[1], o[2]) != (0, 0)] + plane_offsets
    barrier = pltpu.get_barrier_semaphore()
    for o in partners:
        pl.semaphore_signal(barrier, inc=1, device_id=at(*o), device_id_type=MESH)

    for load in loads:
        load.wait()

    low_tab = jnp.broadcast_to(table[0:1, :], (8, 128))
    high_tab = jnp.broadcast_to(table[1:2, :], (8, 128))

    def look(index):
        lane = index & 127
        low = jnp.take_along_axis(low_tab, lane, axis=1, mode="promise_in_bounds")
        high = jnp.take_along_axis(high_tab, lane, axis=1, mode="promise_in_bounds")
        return jnp.where(index >= 128, high, low)

    for p in range(2):
        slope = look(bins[p]) * (1.0 - frac[p]) + look(bins[p] + 1) * frac[p]
        st[13, p] = st[13, p] + (slope - SHIFT)

    pl.semaphore_wait(barrier, len(partners))

    lane = lax.broadcasted_iota(jnp.int32, (16, 128), 1)
    from_right = lane < 64

    def exchange(it):
        for dx, dy, dz in OFFSETS:
            src_p, dst_p, n_p = {0: (0, 0, 2), 1: (1, 3, 1), -1: (0, 2, 1)}[dx]
            src_y, dst_y, n_y = {0: (0, 0, 8), 1: (7, 15, 1), -1: (0, 8, 1)}[dy]
            side = {0: 0, 1: 2, -1: 1}[dz]
            pltpu.make_async_remote_copy(
                src_ref=halo.at[it, pl.ds(src_p, n_p), 0, pl.ds(src_y, n_y), :],
                dst_ref=halo.at[it, pl.ds(dst_p, n_p), side, pl.ds(dst_y, n_y), :],
                send_sem=send_sem.at[0],
                recv_sem=halo_sem.at[it],
                device_id=at(dx, dy, dz),
                device_id_type=MESH,
            ).start()
        pltpu.make_async_copy(halo_bytes, halo_bytes, halo_sem.at[it]).wait()

    def apply(it):
        total = [jnp.zeros((8, 128), jnp.float32) for _ in range(2)]
        for slot, plane in ((0, 0), (1, 1), (2, 2), (3, -1)):
            side = jnp.where(from_right, halo[it, slot, 1], halo[it, slot, 2])
            wide = jnp.concatenate([halo[it, slot, 0], side], axis=1)
            for b in (-1, 0, 1):
                rows = wide if b == 0 else pltpu.roll(wide, (-b) % 16, 0)
                rows = rows[0:8]
                for c in (-1, 0, 1):
                    moved = rows if c == 0 else pltpu.roll(rows, (-c) % 256, 1)
                    moved = moved[:, 0:128]
                    for p in range(2):
                        a = plane - p
                        if -1 <= a <= 1:
                            total[p] = total[p] + st[9 * (a + 1) + 3 * (b + 1) + (c + 1), p] * moved
        return total

    v = [[halo[0, p, 0, 0:8, :] for p in range(2)]]
    for it in range(3):
        exchange(it)
        new = apply(it)
        if it < 2:
            for p in range(2):
                halo[it + 1, p, 0, 0:8, :] = new[p]
        v.append(new)

    row_id = lax.broadcasted_iota(jnp.int32, (8, 128), 0)
    lane_id = lax.broadcasted_iota(jnp.int32, (8, 128), 1)
    tile = jnp.zeros((8, 128), jnp.float32)
    for k in range(6):
        i, j = k // 2, (k + 1) // 2
        product = v[i][0] * v[j][0] + v[i][1] * v[j][1]
        tile = jnp.where(row_id == k, jnp.sum(product, axis=0, keepdims=True), tile)
    for shift in (64, 32, 16):
        tile = tile + pltpu.roll(tile, shift, 1)
    row = jnp.sum(jnp.where((lane_id >> 4) == row_id, tile, 0.0), axis=0, keepdims=True)

    def spread(rows, here, offsets, sem):
        for o in offsets:
            pltpu.make_async_remote_copy(
                src_ref=rows.at[here],
                dst_ref=rows.at[here],
                send_sem=send_sem.at[0],
                recv_sem=sem,
                device_id=at(*o),
                device_id_type=MESH,
            ).start()
        count = len(offsets)
        pltpu.make_async_copy(rows.at[0:count], rows.at[0:count], sem).wait()

    here = gy * GZ + gz
    plane_rows[here] = row
    spread(plane_rows, here, plane_offsets, plane_sem.at[0])
    terms = [plane_rows[k] for k in range(PLANE)]
    while len(terms) > 1:
        terms = [terms[k] + terms[k + 1] for k in range(0, len(terms), 2)]
    line_rows[gx] = terms[0]
    spread(line_rows, gx, line_offsets, line_sem.at[0])
    terms = [(line_rows[k], None) for k in range(GX)]
    terms = [two_sum(terms[k][0], terms[k + 1][0]) for k in range(0, GX, 2)]
    while len(terms) > 1:
        terms = [pair_add(terms[k], terms[k + 1]) for k in range(0, len(terms), 2)]
    pair = terms[0]
    for shift in (8, 4, 2, 1):
        pair = pair_add(pair, (pltpu.roll(pair[0], shift, 1), pltpu.roll(pair[1], shift, 1)))

    moments = [
        tuple(jnp.broadcast_to(part[:, 16 * k + 15 : 16 * k + 16], (8, 128)) for part in pair)
        for k in range(6)
    ]
    tau, x_coef, r_coef = conjugate(moments)
    for p in range(2):
        level = [v[k][p] for k in range(4)]
        basis = [level[0]]
        while len(level) > 1:
            level = [level[k + 1] - tau * level[k] for k in range(len(level) - 1)]
            basis.append(level[0])
        x_out[p] = x_coef[0] * basis[0] + x_coef[1] * basis[1] + x_coef[2] * basis[2]
        r_out[p] = (
            r_coef[0] * basis[0] + r_coef[1] * basis[1] + r_coef[2] * basis[2] + r_coef[3] * basis[3]
        )

    for it in range(3):
        pltpu.make_async_copy(halo_bytes, halo_bytes, send_sem.at[0]).wait()
    for rows, count in ((plane_rows, PLANE - 1), (line_rows, GX - 1)):
        pltpu.make_async_copy(rows.at[0:count], rows.at[0:count], send_sem.at[0]).wait()


def local(right_side, stencil, cool_table, cool_bin, cool_frac):
    block = jax.ShapeDtypeStruct((2, 8, 128), jnp.float32)
    return pl.pallas_call(
        kernel,
        out_shape=(block, block),
        in_specs=[pl.BlockSpec(memory_space=pl.ANY)] * 5,
        out_specs=[pl.BlockSpec(memory_space=pltpu.VMEM)] * 2,
        scratch_shapes=[
            pltpu.VMEM((27, 2, 8, 128), jnp.float32),
            pltpu.VMEM((3, 4, 3, 16, 128), jnp.float32),
            pltpu.VMEM((2, 128), jnp.float32),
            pltpu.VMEM((2, 8, 128), jnp.int32),
            pltpu.VMEM((2, 8, 128), jnp.float32),
            pltpu.VMEM((PLANE, 1, 128), jnp.float32),
            pltpu.VMEM((GX, 1, 128), jnp.float32),
            pltpu.SemaphoreType.DMA((5,)),
            pltpu.SemaphoreType.DMA((1,)),
            pltpu.SemaphoreType.DMA((3,)),
            pltpu.SemaphoreType.DMA((1,)),
            pltpu.SemaphoreType.DMA((1,)),
            pltpu.VMEM((104, 128), jnp.float32),
        ],
        compiler_params=pltpu.CompilerParams(
            collective_id=0, has_side_effects=True, vmem_limit_bytes=60 << 20
        ),
    )(right_side, stencil, cool_table.reshape(2, 128), cool_bin, cool_frac)


def solution(mesh):
    block = P("gx", "gy", "gz")
    return jax.shard_map(
        local,
        mesh=mesh,
        in_specs=(block, P(None, "gx", "gy", "gz"), P(), block, block),
        out_specs=(block, block),
        check_vma=False,
    )
```

time: 867 us -> 62.1 us (0.07)
  blocking collectives: 770 us -> 0 us
  starting transfers between devices: 64.2 us -> 0 us
  Pallas kernels: 0 us -> 59.4 us
  waiting for transfers between devices: 14 us -> 0 us
    psum x5 -> x0, blocking collectives: 770 us -> none  [the longest x3 457 us: squares(): return lax.psum(jnp.sum(residual * residual), ('gx', 'gy', 'gz'))]
    ppermute x18 -> x0, starting transfers between devices: 64.2 us -> none  [the longest x9 34.2 us: padded_2(): lax.ppermute(lax.slice_in_dim(block, 0, width, axis=dim), axis, backward)]
    pallas_call x0 -> x1, Pallas kernels: none -> 59.4 us  [local(): pl.pallas_call(kernel, out_shape=(block, block), in_specs=[pl.BlockSpec(m...]
    ppermute x18 -> x0, waiting for transfers between devices: 14 us -> none  [the longest x9 11.9 us: padded_2(): lax.ppermute(lax.slice_in_dim(block, 0, width, axis=dim), axis, backward)]
  transfers between devices with their start and end apart: 18 -> 0, of which waited for: 10 -> 0; matrix products, arithmetic and copies ran while one was open for 1% -> 0% of each run, Pallas kernels for 0% -> 0%
where the time goes in v1:
time: 62.1 us; the launch traced here: 61.9 us
  Pallas kernels  59.4 us (96%)
  local copies, waits for them, and re-layouts  1.9 us (3%)
  between operations  0.65 us (1%)
    pallas_call x1, Pallas kernels, local(): pl.pallas_call(kernel, out_shape=(block, block), in_specs=[pl.BlockSpec(m...  59.4 us
    unnamed x4, local copies, waits for them, and re-layouts  1.9 us

profile of v1, /device:TPU:1, one launch (start us, length us, event | category | flops | bytes accessed | tf_op | source)
XLA Modules:
  0.0 61.9 jit_solution(7526182998382267017)
XLA Ops:
  0.6 59.4 %shard_map.68 = (f32[2,8,128]{2,1,0:T(8,128)}, f32[2,8,128]{2,1,0:T(8,128)}) custom-call(f32[2,8,128]{2,1,0:T(8,128)} %rhs_hbm.1, f32[27,2,8,128]{3,2,1,0:T(8,128)} %stencil_hbm.1, f32[2,128]{1,0:T(2,128)} %bitcast.1, s32[2,8,128]{2,1,0:T(8,128)} %bin_hbm.1, f32[2,8,128]{2,1,0:T(8,128)} %frac_hbm.1), custom_call_target="tpu_custom_call" | custom-call | tf_op jit(solution)/shard_map/pallas_call | solution.py:261
  60.0 0.0 copy-start
  60.0 1.3 %copy.9 = f32[2,8,128]{2,1,0:T(8,128)} copy(f32[2,8,128]{2,1,0:T(8,128)} %get-tuple-element.4) | data formatting | bytes 16384
  61.3 0.0 copy-done
  61.3 0.6 copy.10
Async XLA Ops:
  60.0 1.3 %copy-start = (f32[2,8,128]{2,1,0:T(8,128)S(1)}, f32[2,8,128]{2,1,0:T(8,128)}, u32[]{:S(2)}) copy-start(f32[2,8,128]{2,1,0:T(8,128)} %get-tuple-element.5) | copy-start | bytes 24580

commit v2 on v1

--- a/solution.py
+++ b/solution.py
@@ -10,13 +10,12 @@
 GX, GY, GZ = 32, 4, 8
 PLANE = GY * GZ
 SHIFT = 4.5
-OFFSETS = [
-    (a, b, c)
-    for a in (-1, 0, 1)
-    for b in (-1, 0, 1)
-    for c in (-1, 0, 1)
-    if (a, b, c) != (0, 0, 0)
-]
+NEAR = [(b, c) for b in (-1, 0, 1) for c in (-1, 0, 1)]
+FIELD_ROWS = {0: (0, 0, 8), 1: (5, 13, 3), -1: (0, 8, 3)}
+COEF_ROWS = {0: (0, 0, 8), 1: (6, 14, 2), -1: (0, 8, 2)}
+FIELD_PLANES = {0: (3, 3, 2), 1: (3, 1, 2), -1: (3, 5, 2), 2: (4, 0, 1), -2: (3, 7, 1)}
+COEF_PLANES = {0: (2, 2), 1: (2, 0), -1: (2, 4)}
+SIDE = {0: 0, 1: 2, -1: 1}
 
 
 def two_sum(a, b):
@@ -103,8 +102,8 @@
 
 def kernel(
     rhs_hbm, stencil_hbm, table_hbm, bin_hbm, frac_hbm, x_out, r_out,
-    st, halo, table, bins, frac, plane_rows, line_rows,
-    in_sem, send_sem, halo_sem, plane_sem, line_sem, halo_bytes,
+    coef, packed, edge, field, moved, table, bins, frac, plane_rows, line_rows,
+    in_sem, send_sem, field_sem, edge_sem, coef_sem, face_sem, plane_sem, line_sem,
 ):
     gx, gy, gz = lax.axis_index("gx"), lax.axis_index("gy"), lax.axis_index("gz")
 
@@ -116,8 +115,8 @@
         )
 
     loads = [
-        pltpu.make_async_copy(rhs_hbm, halo.at[0, 0:2, 0, 0:8, :], in_sem.at[0]),
-        pltpu.make_async_copy(stencil_hbm, st, in_sem.at[1]),
+        pltpu.make_async_copy(rhs_hbm, field.at[0, 3:5, 0:8, :], in_sem.at[0]),
+        pltpu.make_async_copy(stencil_hbm, coef.at[:, 2:4, 0:8, 0:128], in_sem.at[1]),
         pltpu.make_async_copy(table_hbm, table, in_sem.at[2]),
         pltpu.make_async_copy(bin_hbm, bins, in_sem.at[3]),
         pltpu.make_async_copy(frac_hbm, frac, in_sem.at[4]),
@@ -127,7 +126,11 @@
 
     plane_offsets = [(0, b, c) for b in range(GY) for c in range(GZ) if (b, c) != (0, 0)]
     line_offsets = [(a, 0, 0) for a in [16] + [k * e for k in range(15, 0, -1) for e in (1, -1)]]
-    partners = line_offsets + [o for o in OFFSETS if o[0] != 0 and (o[1], o[2]) != (0, 0)] + plane_offsets
+    partners = (
+        line_offsets
+        + [(a, b, c) for a in (-2, 2, -1, 1) for b, c in NEAR if (b, c) != (0, 0)]
+        + plane_offsets
+    )
     barrier = pltpu.get_barrier_semaphore()
     for o in partners:
         pl.semaphore_signal(barrier, inc=1, device_id=at(*o), device_id_type=MESH)
@@ -144,58 +147,120 @@
         high = jnp.take_along_axis(high_tab, lane, axis=1, mode="promise_in_bounds")
         return jnp.where(index >= 128, high, low)
 
+    row_id = lax.broadcasted_iota(jnp.int32, (8, 128), 0)
+    lane_id = lax.broadcasted_iota(jnp.int32, (8, 128), 1)
     for p in range(2):
         slope = look(bins[p]) * (1.0 - frac[p]) + look(bins[p] + 1) * frac[p]
-        st[13, p] = st[13, p] + (slope - SHIFT)
+        coef[13, 2 + p, 0:8, 0:128] = coef[13, 2 + p, 0:8, 0:128] + (slope - SHIFT)
+        tile = jnp.zeros((8, 128), jnp.float32)
+        for k in range(27):
+            turned = pltpu.roll(coef[k, 2 + p, 0:8, 0:128], (4 * k + 2) % 128, 1)
+            tile = jnp.where((lane_id >> 2) == k, turned, tile)
+        packed[p] = tile
 
     pl.semaphore_wait(barrier, len(partners))
 
-    lane = lax.broadcasted_iota(jnp.int32, (16, 128), 1)
-    from_right = lane < 64
-
-    def exchange(it):
-        for dx, dy, dz in OFFSETS:
-            src_p, dst_p, n_p = {0: (0, 0, 2), 1: (1, 3, 1), -1: (0, 2, 1)}[dx]
-            src_y, dst_y, n_y = {0: (0, 0, 8), 1: (7, 15, 1), -1: (0, 8, 1)}[dy]
-            side = {0: 0, 1: 2, -1: 1}[dz]
-            pltpu.make_async_remote_copy(
-                src_ref=halo.at[it, pl.ds(src_p, n_p), 0, pl.ds(src_y, n_y), :],
-                dst_ref=halo.at[it, pl.ds(dst_p, n_p), side, pl.ds(dst_y, n_y), :],
-                send_sem=send_sem.at[0],
-                recv_sem=halo_sem.at[it],
-                device_id=at(dx, dy, dz),
-                device_id_type=MESH,
-            ).start()
-        pltpu.make_async_copy(halo_bytes, halo_bytes, halo_sem.at[it]).wait()
-
-    def apply(it):
-        total = [jnp.zeros((8, 128), jnp.float32) for _ in range(2)]
-        for slot, plane in ((0, 0), (1, 1), (2, 2), (3, -1)):
-            side = jnp.where(from_right, halo[it, slot, 1], halo[it, slot, 2])
-            wide = jnp.concatenate([halo[it, slot, 0], side], axis=1)
-            for b in (-1, 0, 1):
-                rows = wide if b == 0 else pltpu.roll(wide, (-b) % 16, 0)
-                rows = rows[0:8]
-                for c in (-1, 0, 1):
-                    moved = rows if c == 0 else pltpu.roll(rows, (-c) % 256, 1)
-                    moved = moved[:, 0:128]
-                    for p in range(2):
-                        a = plane - p
-                        if -1 <= a <= 1:
-                            total[p] = total[p] + st[9 * (a + 1) + 3 * (b + 1) + (c + 1), p] * moved
+    def send(src, dst, sem, o):
+        pltpu.make_async_remote_copy(
+            src_ref=src, dst_ref=dst, send_sem=send_sem.at[0], recv_sem=sem,
+            device_id=at(*o), device_id_type=MESH,
+        ).start()
+
+    def send_field(dx, dy, dz):
+        p_src, p_dst, p_n = FIELD_PLANES[dx]
+        y_src, y_dst, y_n = FIELD_ROWS[dy]
+        send(
+            field.at[0, pl.ds(p_src, p_n), pl.ds(y_src, y_n), :],
+            field.at[SIDE[dz], pl.ds(p_dst, p_n), pl.ds(y_dst, y_n), :],
+            field_sem.at[0], (dx, dy, dz),
+        )
+
+    def send_edge(dx, dy, dz):
+        p_src, p_dst = COEF_PLANES[dx]
+        y_src, y_dst, y_n = COEF_ROWS[dy]
+        send(
+            packed.at[:, pl.ds(y_src, y_n), :],
+            edge.at[SIDE[dz] - 1, pl.ds(p_dst, 2), pl.ds(y_dst, y_n), :],
+            edge_sem.at[0], (dx, dy, dz),
+        )
+
+    def send_coef(dx, dy, first, count, sem):
+        p_src, p_dst = COEF_PLANES[dx]
+        y_src, y_dst, y_n = COEF_ROWS[dy]
+        send(
+            coef.at[pl.ds(first, count), pl.ds(p_src, 2), pl.ds(y_src, y_n), 0:128],
+            coef.at[pl.ds(first, count), pl.ds(p_dst, 2), pl.ds(y_dst, y_n), 0:128],
+            sem, (dx, dy, 0),
+        )
+
+    offsets = [(a, b, c) for a in (-1, 1, -2, 2, 0) for b, c in NEAR if (a, b, c) != (0, 0, 0)]
+    offsets.sort(key=lambda o: -sum(abs(d) for d in o))
+    for o in offsets:
+        send_field(*o)
+        if o[2] != 0 and abs(o[0]) <= 1:
+            send_edge(*o)
+    for dx in (-1, 1):
+        for dy in (-1, 1):
+            send_coef(dx, dy, 0, 27, coef_sem.at[0])
+    send_coef(1, 0, 0, 14, face_sem.at[0])
+    send_coef(-1, 0, 13, 14, face_sem.at[0])
+    for dy in (-1, 1):
+        send_coef(0, dy, 0, 27, coef_sem.at[0])
+
+    field_bytes = coef.at[0:20, 0, :, 0:128]
+    edge_bytes = coef.at[0:9, 0, :, 0:128]
+    coef_bytes = coef.at[0:27, 0:3, 0:8, 0:128]
+    face_bytes = coef.at[0:14, 0:2, :, 0:128]
+
+    def moved_by(array, b, c):
+        if b:
+            array = pltpu.roll(array, (-b) % 16, 1)
+        if c:
+            array = pltpu.roll(array, (-c) % 256, 2)
+        return array
+
+    def turn(array, planes):
+        for n, (b, c) in enumerate(NEAR):
+            moved[n, 0:planes] = moved_by(array, b, c)
+
+    def apply(planes, first):
+        total = jnp.zeros((planes, 16, 256), jnp.float32)
+        for k in range(27):
+            a = k // 9
+            total = total + coef[k, first : first + planes] * moved[k % 9, a : a + planes]
         return total
 
-    v = [[halo[0, p, 0, 0:8, :] for p in range(2)]]
-    for it in range(3):
-        exchange(it)
-        new = apply(it)
-        if it < 2:
-            for p in range(2):
-                halo[it + 1, p, 0, 0:8, :] = new[p]
-        v.append(new)
-
-    row_id = lax.broadcasted_iota(jnp.int32, (8, 128), 0)
-    lane_id = lax.broadcasted_iota(jnp.int32, (8, 128), 1)
+    pltpu.make_async_copy(field_bytes, field_bytes, field_sem.at[0]).wait()
+    lane_wide = lax.broadcasted_iota(jnp.int32, (8, 16, 128), 2)
+    side = jnp.where(lane_wide < 64, field[1], field[2])
+    turn(jnp.concatenate([field[0], side], axis=2), 8)
+
+    pltpu.make_async_copy(edge_bytes, edge_bytes, edge_sem.at[0]).wait()
+    merged = jnp.where((lane_wide[0:6] & 3) < 2, edge[1], edge[0])
+    for k in range(27):
+        coef[k, :, :, 128:256] = pltpu.roll(merged, (126 - 4 * k) % 128, 2)
+
+    pltpu.make_async_copy(coef_bytes, coef_bytes, coef_sem.at[0]).wait()
+    pltpu.make_async_copy(face_bytes, face_bytes, face_sem.at[0]).wait()
+    for k in range(27):
+        if k == 13:
+            continue
+        a, b, c = k // 9 - 1, k // 3 % 3 - 1, k % 3 - 1
+        first = 0 if k > 13 else 4
+        mirror = moved_by(coef[26 - k, first + a : first + a + 2], b, c)
+        coef[k, first : first + 2, 0:8, 0:128] = mirror[:, 0:8, 0:128]
+
+    one = apply(6, 0)
+    turn(one, 6)
+    two = apply(4, 1)
+    turn(two, 4)
+    three = jnp.zeros((2, 8, 128), jnp.float32)
+    for k in range(27):
+        a = k // 9
+        three = three + coef[k, 2:4, 0:8, 0:128] * moved[k % 9, a : a + 2, 0:8, 0:128]
+    own = [field[0, 3:5, 0:8, :], one[2:4, 0:8, 0:128], two[1:3, 0:8, 0:128], three]
+    v = [[array[p] for p in range(2)] for array in own]
+
     tile = jnp.zeros((8, 128), jnp.float32)
     for k in range(6):
         i, j = k // 2, (k + 1) // 2
@@ -250,8 +315,8 @@
             r_coef[0] * basis[0] + r_coef[1] * basis[1] + r_coef[2] * basis[2] + r_coef[3] * basis[3]
         )
 
-    for it in range(3):
-        pltpu.make_async_copy(halo_bytes, halo_bytes, send_sem.at[0]).wait()
+    for size in (field_bytes, edge_bytes, coef_bytes, face_bytes):
+        pltpu.make_async_copy(size, size, send_sem.at[0]).wait()
     for rows, count in ((plane_rows, PLANE - 1), (line_rows, GX - 1)):
         pltpu.make_async_copy(rows.at[0:count], rows.at[0:count], send_sem.at[0]).wait()
 
@@ -264,20 +329,19 @@
         in_specs=[pl.BlockSpec(memory_space=pl.ANY)] * 5,
         out_specs=[pl.BlockSpec(memory_space=pltpu.VMEM)] * 2,
         scratch_shapes=[
-            pltpu.VMEM((27, 2, 8, 128), jnp.float32),
-            pltpu.VMEM((3, 4, 3, 16, 128), jnp.float32),
+            pltpu.VMEM((27, 6, 16, 256), jnp.float32),
+            pltpu.VMEM((2, 8, 128), jnp.float32),
+            pltpu.VMEM((2, 6, 16, 128), jnp.float32),
+            pltpu.VMEM((3, 8, 16, 128), jnp.float32),
+            pltpu.VMEM((9, 8, 16, 256), jnp.float32),
             pltpu.VMEM((2, 128), jnp.float32),
             pltpu.VMEM((2, 8, 128), jnp.int32),
             pltpu.VMEM((2, 8, 128), jnp.float32),
             pltpu.VMEM((PLANE, 1, 128), jnp.float32),
             pltpu.VMEM((GX, 1, 128), jnp.float32),
             pltpu.SemaphoreType.DMA((5,)),
-            pltpu.SemaphoreType.DMA((1,)),
-            pltpu.SemaphoreType.DMA((3,)),
-            pltpu.SemaphoreType.DMA((1,)),
-            pltpu.SemaphoreType.DMA((1,)),
-            pltpu.VMEM((104, 128), jnp.float32),
-        ],
+        ]
+        + [pltpu.SemaphoreType.DMA((1,))] * 7,
         compiler_params=pltpu.CompilerParams(
             collective_id=0, has_side_effects=True, vmem_limit_bytes=60 << 20
         ),

time: 62.1 us -> 58.9 us (0.948)
  Pallas kernels: 59.4 us -> 56.2 us
    pallas_call x1, Pallas kernels: 59.4 us -> 56.2 us  [local(): pl.pallas_call(kernel, out_shape=(block, block), in_specs=[pl.BlockSpec(m...]
where the time goes in v2:
time: 58.9 us; the launch traced here: 58.7 us
  Pallas kernels  56.2 us (95%)
  local copies, waits for them, and re-layouts  1.9 us (3%)
  between operations  0.65 us (1%)
    pallas_call x1, Pallas kernels, local(): pl.pallas_call(kernel, out_shape=(block, block), in_specs=[pl.BlockSpec(m...  56.2 us
    unnamed x4, local copies, waits for them, and re-layouts  1.9 us

profile of v2, /device:TPU:1, one launch (start us, length us, event | category | flops | bytes accessed | tf_op | source)
XLA Modules:
  0.0 58.7 jit_solution(12354918506511319942)
XLA Ops:
  0.6 56.2 %shard_map.68 = (f32[2,8,128]{2,1,0:T(8,128)}, f32[2,8,128]{2,1,0:T(8,128)}) custom-call(f32[2,8,128]{2,1,0:T(8,128)} %rhs_hbm.1, f32[27,2,8,128]{3,2,1,0:T(8,128)} %stencil_hbm.1, f32[2,128]{1,0:T(2,128)} %bitcast.1, s32[2,8,128]{2,1,0:T(8,128)} %bin_hbm.1, f32[2,8,128]{2,1,0:T(8,128)} %frac_hbm.1), custom_call_target="tpu_custom_call" | custom-call | tf_op jit(solution)/shard_map/pallas_call | solution.py:326
  56.8 0.0 copy-start
  56.8 1.3 %copy.9 = f32[2,8,128]{2,1,0:T(8,128)} copy(f32[2,8,128]{2,1,0:T(8,128)} %get-tuple-element.4) | data formatting | bytes 16384
  58.1 0.0 copy-done
  58.1 0.6 %copy.10 = f32[2,8,128]{2,1,0:T(8,128)} copy(f32[2,8,128]{2,1,0:T(8,128)S(1)} %copy-done) | data formatting | bytes 16384
Async XLA Ops:
  56.8 1.3 %copy-start = (f32[2,8,128]{2,1,0:T(8,128)S(1)}, f32[2,8,128]{2,1,0:T(8,128)}, u32[]{:S(2)}) copy-start(f32[2,8,128]{2,1,0:T(8,128)} %get-tuple-element.5) | copy-start | bytes 24580

commit v3 on v2

--- a/solution.py
+++ b/solution.py
@@ -101,9 +101,10 @@
 
 
 def kernel(
-    rhs_hbm, stencil_hbm, table_hbm, bin_hbm, frac_hbm, x_out, r_out,
+    rhs_hbm, stencil_hbm, table_hbm, bin_hbm, frac_hbm, out,
     coef, packed, edge, field, moved, table, bins, frac, plane_rows, line_rows,
     in_sem, send_sem, field_sem, edge_sem, coef_sem, face_sem, plane_sem, line_sem,
+    relay_4, relay_8,
 ):
     gx, gy, gz = lax.axis_index("gx"), lax.axis_index("gy"), lax.axis_index("gz")
 
@@ -126,11 +127,9 @@
 
     plane_offsets = [(0, b, c) for b in range(GY) for c in range(GZ) if (b, c) != (0, 0)]
     line_offsets = [(a, 0, 0) for a in [16] + [k * e for k in range(15, 0, -1) for e in (1, -1)]]
-    partners = (
-        line_offsets
-        + [(a, b, c) for a in (-2, 2, -1, 1) for b, c in NEAR if (b, c) != (0, 0)]
-        + plane_offsets
-    )
+    around = [(a, b, c) for a in (-2, 2, -1, 1) for b, c in NEAR if (b, c) != (0, 0)]
+    around.sort(key=lambda o: -sum(abs(d) for d in o))
+    partners = around + plane_offsets + [(a, 0, 0) for a in (4, -4, 3, -3, 2, -2, 1, -1)]
     barrier = pltpu.get_barrier_semaphore()
     for o in partners:
         pl.semaphore_signal(barrier, inc=1, device_id=at(*o), device_id_type=MESH)
@@ -159,6 +158,9 @@
         packed[p] = tile
 
     pl.semaphore_wait(barrier, len(partners))
+
+    for a in (4, -4):
+        pl.semaphore_signal(relay_4, inc=1, device_id=at(a, 0, 0), device_id_type=MESH)
 
     def send(src, dst, sem, o):
         pltpu.make_async_remote_copy(
@@ -207,6 +209,10 @@
     for dy in (-1, 1):
         send_coef(0, dy, 0, 27, coef_sem.at[0])
 
+    pl.semaphore_wait(relay_4, 2)
+    for a in (8, -8):
+        pl.semaphore_signal(relay_8, inc=1, device_id=at(a, 0, 0), device_id_type=MESH)
+
     field_bytes = coef.at[0:20, 0, :, 0:128]
     edge_bytes = coef.at[0:9, 0, :, 0:128]
     coef_bytes = coef.at[0:27, 0:3, 0:8, 0:128]
@@ -290,6 +296,7 @@
     while len(terms) > 1:
         terms = [terms[k] + terms[k + 1] for k in range(0, len(terms), 2)]
     line_rows[gx] = terms[0]
+    pl.semaphore_wait(relay_8, 2)
     spread(line_rows, gx, line_offsets, line_sem.at[0])
     terms = [(line_rows[k], None) for k in range(GX)]
     terms = [two_sum(terms[k][0], terms[k + 1][0]) for k in range(0, GX, 2)]
@@ -310,8 +317,8 @@
         while len(level) > 1:
             level = [level[k + 1] - tau * level[k] for k in range(len(level) - 1)]
             basis.append(level[0])
-        x_out[p] = x_coef[0] * basis[0] + x_coef[1] * basis[1] + x_coef[2] * basis[2]
-        r_out[p] = (
+        out[p] = x_coef[0] * basis[0] + x_coef[1] * basis[1] + x_coef[2] * basis[2]
+        out[2 + p] = (
             r_coef[0] * basis[0] + r_coef[1] * basis[1] + r_coef[2] * basis[2] + r_coef[3] * basis[3]
         )
 
@@ -322,12 +329,11 @@
 
 
 def local(right_side, stencil, cool_table, cool_bin, cool_frac):
-    block = jax.ShapeDtypeStruct((2, 8, 128), jnp.float32)
-    return pl.pallas_call(
+    both = pl.pallas_call(
         kernel,
-        out_shape=(block, block),
+        out_shape=jax.ShapeDtypeStruct((4, 8, 128), jnp.float32),
         in_specs=[pl.BlockSpec(memory_space=pl.ANY)] * 5,
-        out_specs=[pl.BlockSpec(memory_space=pltpu.VMEM)] * 2,
+        out_specs=pl.BlockSpec(memory_space=pltpu.VMEM),
         scratch_shapes=[
             pltpu.VMEM((27, 6, 16, 256), jnp.float32),
             pltpu.VMEM((2, 8, 128), jnp.float32),
@@ -341,11 +347,13 @@
             pltpu.VMEM((GX, 1, 128), jnp.float32),
             pltpu.SemaphoreType.DMA((5,)),
         ]
-        + [pltpu.SemaphoreType.DMA((1,))] * 7,
+        + [pltpu.SemaphoreType.DMA((1,))] * 7
+        + [pltpu.SemaphoreType.REGULAR] * 2,
         compiler_params=pltpu.CompilerParams(
             collective_id=0, has_side_effects=True, vmem_limit_bytes=60 << 20
         ),
     )(right_side, stencil, cool_table.reshape(2, 128), cool_bin, cool_frac)
+    return both[0:2], both[2:4]
 
 
 def solution(mesh):

time: 58.9 us -> 53.9 us (0.915)
  Pallas kernels: 56.2 us -> 51.7 us
    pallas_call x1, Pallas kernels: 56.2 us -> 51.7 us  [local(): pl.pallas_call(kernel, out_shape=jax.ShapeDtypeStruct((4, 8, 128), jnp.fl...]
    unnamed x4 -> x0, local copies, waits for them, and re-layouts: 1.9 us -> none
    slice x0 -> x1, local copies, waits for them, and re-layouts: none -> 1.32 us  [local(): return (both[0:2], both[2:4])]
where the time goes in v3:
time: 53.9 us; the launch traced here: 53.7 us
  Pallas kernels  51.7 us (96%)
  local copies, waits for them, and re-layouts  1.32 us (2%)
  between operations  0.64 us (1%)
    pallas_call x1, Pallas kernels, local(): pl.pallas_call(kernel, out_shape=jax.ShapeDtypeStruct((4, 8, 128), jnp.fl...  51.7 us
    slice x1, local copies, waits for them, and re-layouts, local(): return (both[0:2], both[2:4])  1.32 us

profile of v3, /device:TPU:1, one launch (start us, length us, event | category | flops | bytes accessed | tf_op | source)
XLA Modules:
  0.0 53.7 jit_solution(683161025959698799)
XLA Ops:
  0.6 51.7 %shard_map.68 = f32[4,8,128]{2,1,0:T(8,128)} custom-call(f32[2,8,128]{2,1,0:T(8,128)} %rhs_hbm.1, f32[27,2,8,128]{3,2,1,0:T(8,128)} %stencil_hbm.1, f32[2,128]{1,0:T(2,128)} %bitcast.1, s32[2,8,128]{2,1,0:T(8,128)} %bin_hbm.1, f32[2,8,128]{2,1,0:T(8,128)} %frac_hbm.1), custom_call_target="tpu_custom_call" | custom-call | tf_op jit(solution)/shard_map/pallas_call | solution.py:332
  52.4 1.3 %fusion = (f32[2,8,128]{2,1,0:T(8,128)}, f32[2,8,128]{2,1,0:T(8,128)}) fusion(f32[4,8,128]{2,1,0:T(8,128)} %shard_map.68), kind=kLoop, calls=%fused_computation | loop fusion | bytes 32768 | tf_op jit(solution)/shard_map/slice | solution.py:356

commit v4 on v3

--- a/solution.py
+++ b/solution.py
@@ -16,6 +16,7 @@
 FIELD_PLANES = {0: (3, 3, 2), 1: (3, 1, 2), -1: (3, 5, 2), 2: (4, 0, 1), -2: (3, 7, 1)}
 COEF_PLANES = {0: (2, 2), 1: (2, 0), -1: (2, 4)}
 SIDE = {0: 0, 1: 2, -1: 1}
+OUTWARD = {(1, -1): (15, 24), (1, 1): (18,), (-1, -1): (6,), (-1, 1): (0, 9)}
 
 
 def two_sum(a, b):
@@ -102,7 +103,7 @@
 
 def kernel(
     rhs_hbm, stencil_hbm, table_hbm, bin_hbm, frac_hbm, out,
-    coef, packed, edge, field, moved, table, bins, frac, plane_rows, line_rows,
+    coef, packed, edge, field, side, own_strip, strips, moved, table, bins, frac, plane_rows, line_rows,
     in_sem, send_sem, field_sem, edge_sem, coef_sem, face_sem, plane_sem, line_sem,
     relay_4, relay_8,
 ):
@@ -116,7 +117,7 @@
         )
 
     loads = [
-        pltpu.make_async_copy(rhs_hbm, field.at[0, 3:5, 0:8, :], in_sem.at[0]),
+        pltpu.make_async_copy(rhs_hbm, field.at[3:5, 0:8, :], in_sem.at[0]),
         pltpu.make_async_copy(stencil_hbm, coef.at[:, 2:4, 0:8, 0:128], in_sem.at[1]),
         pltpu.make_async_copy(table_hbm, table, in_sem.at[2]),
         pltpu.make_async_copy(bin_hbm, bins, in_sem.at[3]),
@@ -157,6 +158,14 @@
             tile = jnp.where((lane_id >> 2) == k, turned, tile)
         packed[p] = tile
 
+    strip = jnp.zeros((8, 128), jnp.float32)
+    for p in range(2):
+        ends = jnp.take_along_axis(
+            field[3 + p, 0:8, :], ((lane_id & 7) + 125) & 127, axis=1, mode="promise_in_bounds"
+        )
+        strip = jnp.where((lane_id >> 3) == row_id + 8 * p, ends, strip)
+    own_strip[0] = jnp.sum(strip, axis=0, keepdims=True)
+
     pl.semaphore_wait(barrier, len(partners))
 
     for a in (4, -4):
@@ -169,11 +178,15 @@
         ).start()
 
     def send_field(dx, dy, dz):
+        if dz:
+            place = strips.at[SIDE[dz] - 1, 3 * (2 - dx) + (1 - dy)]
+            send(own_strip.at[0], place, field_sem.at[0], (dx, dy, dz))
+            return
         p_src, p_dst, p_n = FIELD_PLANES[dx]
         y_src, y_dst, y_n = FIELD_ROWS[dy]
         send(
-            field.at[0, pl.ds(p_src, p_n), pl.ds(y_src, y_n), :],
-            field.at[SIDE[dz], pl.ds(p_dst, p_n), pl.ds(y_dst, y_n), :],
+            field.at[pl.ds(p_src, p_n), pl.ds(y_src, y_n), :],
+            field.at[pl.ds(p_dst, p_n), pl.ds(y_dst, y_n), :],
             field_sem.at[0], (dx, dy, dz),
         )
 
@@ -186,9 +199,9 @@
             edge_sem.at[0], (dx, dy, dz),
         )
 
-    def send_coef(dx, dy, first, count, sem):
+    def send_coef(dx, dy, first, count, sem, rows=None):
         p_src, p_dst = COEF_PLANES[dx]
-        y_src, y_dst, y_n = COEF_ROWS[dy]
+        y_src, y_dst, y_n = rows or COEF_ROWS[dy]
         send(
             coef.at[pl.ds(first, count), pl.ds(p_src, 2), pl.ds(y_src, y_n), 0:128],
             coef.at[pl.ds(first, count), pl.ds(p_dst, 2), pl.ds(y_dst, y_n), 0:128],
@@ -202,10 +215,14 @@
         if o[2] != 0 and abs(o[0]) <= 1:
             send_edge(*o)
     for dx in (-1, 1):
+        half = 0 if dx == 1 else 13
         for dy in (-1, 1):
-            send_coef(dx, dy, 0, 27, coef_sem.at[0])
-    send_coef(1, 0, 0, 14, face_sem.at[0])
-    send_coef(-1, 0, 13, 14, face_sem.at[0])
+            send_coef(dx, dy, half, 14, coef_sem.at[0])
+            for first in OUTWARD[dx, dy]:
+                rows = (6, 14, 1) if dy == 1 else (1, 9, 1)
+                send_coef(dx, dy, first, 3, coef_sem.at[0], rows)
+    for dx in (-1, 1):
+        send_coef(dx, 0, 0 if dx == 1 else 13, 14, face_sem.at[0])
     for dy in (-1, 1):
         send_coef(0, dy, 0, 27, coef_sem.at[0])
 
@@ -213,9 +230,9 @@
     for a in (8, -8):
         pl.semaphore_signal(relay_8, inc=1, device_id=at(a, 0, 0), device_id_type=MESH)
 
-    field_bytes = coef.at[0:20, 0, :, 0:128]
+    field_bytes = coef.at[0:9, 0:2, 0:7, 0:128]
     edge_bytes = coef.at[0:9, 0, :, 0:128]
-    coef_bytes = coef.at[0:27, 0:3, 0:8, 0:128]
+    coef_bytes = coef.at[0:17, 0:4, 0:7, 0:128]
     face_bytes = coef.at[0:14, 0:2, :, 0:128]
 
     def moved_by(array, b, c):
@@ -237,24 +254,41 @@
         return total
 
     pltpu.make_async_copy(field_bytes, field_bytes, field_sem.at[0]).wait()
-    lane_wide = lax.broadcasted_iota(jnp.int32, (8, 16, 128), 2)
-    side = jnp.where(lane_wide < 64, field[1], field[2])
-    turn(jnp.concatenate([field[0], side], axis=2), 8)
+    for plane in range(8):
+        dx = (plane - 3) // 2
+        first = 64 * ((plane - 3) % 2)
+        line = lax.broadcasted_iota(jnp.int32, (1, 128), 1)
+
+        def strip_of(dy):
+            n = 3 * (dx + 2) + (dy + 1)
+            return jnp.where((line & 7) < 3, strips[1, n], strips[0, n])
+
+        source = [strip_of(0), jnp.where((line & 63) < 32, strip_of(1), strip_of(-1))]
+        index = first + 8 * row_id + ((lane_id + 3) & 7)
+        for n in range(2):
+            side[plane, 8 * n : 8 * n + 8, :] = jnp.take_along_axis(
+                jnp.broadcast_to(source[n], (8, 128)), index, axis=1, mode="promise_in_bounds"
+            )
+    turn(jnp.concatenate([field[...], side[...]], axis=2), 8)
 
     pltpu.make_async_copy(edge_bytes, edge_bytes, edge_sem.at[0]).wait()
-    merged = jnp.where((lane_wide[0:6] & 3) < 2, edge[1], edge[0])
+    lane_wide = lax.broadcasted_iota(jnp.int32, (6, 16, 128), 2)
+    merged = jnp.where((lane_wide & 3) < 2, edge[1], edge[0])
     for k in range(27):
         coef[k, :, :, 128:256] = pltpu.roll(merged, (126 - 4 * k) % 128, 2)
 
     pltpu.make_async_copy(coef_bytes, coef_bytes, coef_sem.at[0]).wait()
     pltpu.make_async_copy(face_bytes, face_bytes, face_sem.at[0]).wait()
+    row_wide = lax.broadcasted_iota(jnp.int32, (2, 16, 128), 1)
     for k in range(27):
         if k == 13:
             continue
         a, b, c = k // 9 - 1, k // 3 % 3 - 1, k % 3 - 1
         first = 0 if k > 13 else 4
-        mirror = moved_by(coef[26 - k, first + a : first + a + 2], b, c)
-        coef[k, first : first + 2, 0:8, 0:128] = mirror[:, 0:8, 0:128]
+        mirror = moved_by(coef[26 - k, first + a : first + a + 2], b, c)[:, :, 0:128]
+        if b:
+            mirror = jnp.where(row_wide == (9 if b == 1 else 14), coef[k, first : first + 2, :, 0:128], mirror)
+        coef[k, first : first + 2, :, 0:128] = mirror
 
     one = apply(6, 0)
     turn(one, 6)
@@ -264,7 +298,7 @@
     for k in range(27):
         a = k // 9
         three = three + coef[k, 2:4, 0:8, 0:128] * moved[k % 9, a : a + 2, 0:8, 0:128]
-    own = [field[0, 3:5, 0:8, :], one[2:4, 0:8, 0:128], two[1:3, 0:8, 0:128], three]
+    own = [field[3:5, 0:8, :], one[2:4, 0:8, 0:128], two[1:3, 0:8, 0:128], three]
     v = [[array[p] for p in range(2)] for array in own]
 
     tile = jnp.zeros((8, 128), jnp.float32)
@@ -338,7 +372,10 @@
             pltpu.VMEM((27, 6, 16, 256), jnp.float32),
             pltpu.VMEM((2, 8, 128), jnp.float32),
             pltpu.VMEM((2, 6, 16, 128), jnp.float32),
-            pltpu.VMEM((3, 8, 16, 128), jnp.float32),
+            pltpu.VMEM((8, 16, 128), jnp.float32),
+            pltpu.VMEM((8, 16, 128), jnp.float32),
+            pltpu.VMEM((1, 1, 128), jnp.float32),
+            pltpu.VMEM((2, 15, 1, 128), jnp.float32),
             pltpu.VMEM((9, 8, 16, 256), jnp.float32),
             pltpu.VMEM((2, 128), jnp.float32),
             pltpu.VMEM((2, 8, 128), jnp.int32),

time: 53.9 us -> 52 us (0.965)
  Pallas kernels: 51.7 us -> 49.8 us
    pallas_call x1, Pallas kernels: 51.7 us -> 49.8 us  [local(): pl.pallas_call(kernel, out_shape=jax.ShapeDtypeStruct((4, 8, 128), jnp.fl...]
where the time goes in v4:
time: 52 us; the launch traced here: 51.7 us
  Pallas kernels  49.8 us (96%)
  local copies, waits for them, and re-layouts  1.32 us (3%)
  between operations  0.64 us (1%)
    pallas_call x1, Pallas kernels, local(): pl.pallas_call(kernel, out_shape=jax.ShapeDtypeStruct((4, 8, 128), jnp.fl...  49.8 us
    slice x1, local copies, waits for them, and re-layouts, local(): return (both[0:2], both[2:4])  1.32 us

profile of v4, /device:TPU:1, one launch (start us, length us, event | category | flops | bytes accessed | tf_op | source)
XLA Modules:
  0.0 51.7 jit_solution(11448024208914630932)
XLA Ops:
  0.6 49.8 %shard_map.68 = f32[4,8,128]{2,1,0:T(8,128)} custom-call(f32[2,8,128]{2,1,0:T(8,128)} %rhs_hbm.1, f32[27,2,8,128]{3,2,1,0:T(8,128)} %stencil_hbm.1, f32[2,128]{1,0:T(2,128)} %bitcast.1, s32[2,8,128]{2,1,0:T(8,128)} %bin_hbm.1, f32[2,8,128]{2,1,0:T(8,128)} %frac_hbm.1), custom_call_target="tpu_custom_call" | custom-call | tf_op jit(solution)/shard_map/pallas_call | solution.py:366
  50.4 1.3 %fusion = (f32[2,8,128]{2,1,0:T(8,128)}, f32[2,8,128]{2,1,0:T(8,128)}) fusion(f32[4,8,128]{2,1,0:T(8,128)} %shard_map.68), kind=kLoop, calls=%fused_computation | loop fusion | bytes 32768 | tf_op jit(solution)/shard_map/slice | solution.py:393

commit v5 on v4

--- a/solution.py
+++ b/solution.py
@@ -104,7 +104,7 @@
 def kernel(
     rhs_hbm, stencil_hbm, table_hbm, bin_hbm, frac_hbm, out,
     coef, packed, edge, field, side, own_strip, strips, moved, table, bins, frac, plane_rows, line_rows,
-    in_sem, send_sem, field_sem, edge_sem, coef_sem, face_sem, plane_sem, line_sem,
+    in_sem, send_sem, field_sem, edge_sem, coef_sem, face_sem, row_sem, plane_sem, line_sem,
     relay_4, relay_8,
 ):
     gx, gy, gz = lax.axis_index("gx"), lax.axis_index("gy"), lax.axis_index("gz")
@@ -127,6 +127,7 @@
         load.start()
 
     plane_offsets = [(0, b, c) for b in range(GY) for c in range(GZ) if (b, c) != (0, 0)]
+    plane_offsets.sort(key=lambda o: -(min(o[1], GY - o[1]) + min(o[2], GZ - o[2]) / 2))
     line_offsets = [(a, 0, 0) for a in [16] + [k * e for k in range(15, 0, -1) for e in (1, -1)]]
     around = [(a, b, c) for a in (-2, 2, -1, 1) for b, c in NEAR if (b, c) != (0, 0)]
     around.sort(key=lambda o: -sum(abs(d) for d in o))
@@ -214,6 +215,8 @@
         send_field(*o)
         if o[2] != 0 and abs(o[0]) <= 1:
             send_edge(*o)
+    for dy in (-1, 1):
+        send_coef(0, dy, 0, 27, row_sem.at[0])
     for dx in (-1, 1):
         half = 0 if dx == 1 else 13
         for dy in (-1, 1):
@@ -223,8 +226,6 @@
                 send_coef(dx, dy, first, 3, coef_sem.at[0], rows)
     for dx in (-1, 1):
         send_coef(dx, 0, 0 if dx == 1 else 13, 14, face_sem.at[0])
-    for dy in (-1, 1):
-        send_coef(0, dy, 0, 27, coef_sem.at[0])
 
     pl.semaphore_wait(relay_4, 2)
     for a in (8, -8):
@@ -232,7 +233,8 @@
 
     field_bytes = coef.at[0:9, 0:2, 0:7, 0:128]
     edge_bytes = coef.at[0:9, 0, :, 0:128]
-    coef_bytes = coef.at[0:17, 0:4, 0:7, 0:128]
+    coef_bytes = coef.at[0:13, 0:4, 0:5, 0:128]
+    row_bytes = coef.at[0:27, 0, 0:8, 0:128]
     face_bytes = coef.at[0:14, 0:2, :, 0:128]
 
     def moved_by(array, b, c):
@@ -246,11 +248,12 @@
         for n, (b, c) in enumerate(NEAR):
             moved[n, 0:planes] = moved_by(array, b, c)
 
-    def apply(planes, first):
+    def apply(planes, first, base=None):
+        base = first if base is None else base
         total = jnp.zeros((planes, 16, 256), jnp.float32)
         for k in range(27):
             a = k // 9
-            total = total + coef[k, first : first + planes] * moved[k % 9, a : a + planes]
+            total = total + coef[k, first : first + planes] * moved[k % 9, first - base + a : first - base + a + planes]
         return total
 
     pltpu.make_async_copy(field_bytes, field_bytes, field_sem.at[0]).wait()
@@ -276,6 +279,9 @@
     merged = jnp.where((lane_wide & 3) < 2, edge[1], edge[0])
     for k in range(27):
         coef[k, :, :, 128:256] = pltpu.roll(merged, (126 - 4 * k) % 128, 2)
+
+    pltpu.make_async_copy(row_bytes, row_bytes, row_sem.at[0]).wait()
+    middle = apply(2, 2, 0)
 
     pltpu.make_async_copy(coef_bytes, coef_bytes, coef_sem.at[0]).wait()
     pltpu.make_async_copy(face_bytes, face_bytes, face_sem.at[0]).wait()
@@ -290,7 +296,7 @@
             mirror = jnp.where(row_wide == (9 if b == 1 else 14), coef[k, first : first + 2, :, 0:128], mirror)
         coef[k, first : first + 2, :, 0:128] = mirror
 
-    one = apply(6, 0)
+    one = jnp.concatenate([apply(2, 0, 0), middle, apply(2, 4, 0)], axis=0)
     turn(one, 6)
     two = apply(4, 1)
     turn(two, 4)
@@ -356,7 +362,7 @@
             r_coef[0] * basis[0] + r_coef[1] * basis[1] + r_coef[2] * basis[2] + r_coef[3] * basis[3]
         )
 
-    for size in (field_bytes, edge_bytes, coef_bytes, face_bytes):
+    for size in (field_bytes, edge_bytes, row_bytes, coef_bytes, face_bytes):
         pltpu.make_async_copy(size, size, send_sem.at[0]).wait()
     for rows, count in ((plane_rows, PLANE - 1), (line_rows, GX - 1)):
         pltpu.make_async_copy(rows.at[0:count], rows.at[0:count], send_sem.at[0]).wait()
@@ -384,7 +390,7 @@
             pltpu.VMEM((GX, 1, 128), jnp.float32),
             pltpu.SemaphoreType.DMA((5,)),
         ]
-        + [pltpu.SemaphoreType.DMA((1,))] * 7
+        + [pltpu.SemaphoreType.DMA((1,))] * 8
         + [pltpu.SemaphoreType.REGULAR] * 2,
         compiler_params=pltpu.CompilerParams(
             collective_id=0, has_side_effects=True, vmem_limit_bytes=60 << 20

time: 52 us -> 51.9 us (level)
  no operation moved by 1% of the time
where the time goes in v5:
time: 51.9 us; the launch traced here: 51.6 us
  Pallas kernels  49.7 us (96%)
  local copies, waits for them, and re-layouts  1.32 us (3%)
  between operations  0.64 us (1%)
    pallas_call x1, Pallas kernels, local(): pl.pallas_call(kernel, out_shape=jax.ShapeDtypeStruct((4, 8, 128), jnp.fl...  49.7 us
    slice x1, local copies, waits for them, and re-layouts, local(): return (both[0:2], both[2:4])  1.32 us

profile of v5, /device:TPU:1, one launch (start us, length us, event | category | flops | bytes accessed | tf_op | source)
XLA Modules:
  0.0 51.6 jit_solution(12900218077422432412)
XLA Ops:
  0.6 49.7 %shard_map.68 = f32[4,8,128]{2,1,0:T(8,128)} custom-call(f32[2,8,128]{2,1,0:T(8,128)} %rhs_hbm.1, f32[27,2,8,128]{3,2,1,0:T(8,128)} %stencil_hbm.1, f32[2,128]{1,0:T(2,128)} %bitcast.1, s32[2,8,128]{2,1,0:T(8,128)} %bin_hbm.1, f32[2,8,128]{2,1,0:T(8,128)} %frac_hbm.1), custom_call_target="tpu_custom_call" | custom-call | tf_op jit(solution)/shard_map/pallas_call | solution.py:372
  50.3 1.3 %fusion = (f32[2,8,128]{2,1,0:T(8,128)}, f32[2,8,128]{2,1,0:T(8,128)}) fusion(f32[4,8,128]{2,1,0:T(8,128)} %shard_map.68), kind=kLoop, calls=%fused_computation | loop fusion | bytes 32768 | tf_op jit(solution)/shard_map/slice | solution.py:399
